TPU v7x, 32 devices: a whole 2x2x4 slice. The times are simulated.
32 devices in a mesh: site: 8 (over z, x), sector: 4 (over y, core).
Axes of the slice: x: 2, y: 2, z: 4, core: 2. Of those that a mesh axis runs over, the one named last changes fastest.
Arguments:
- site_tensors: bfloat16 [8, 2, 1536, 384], P('site', None, 'sector'), may hold values from -0.21875 to 0.21875
- environments: bfloat16 [8, 5, 1536, 384], P('site', None, 'sector'), may hold values from -6 to 6
- mpo: float32 [8, 5, 5, 2, 2], P('site'), may hold values from -4 to 4
- boundary: bfloat16 [5, 1536, 384], P(None, 'sector'), may hold values from -6 to 6
Outputs:
- environments_out: bfloat16 [8, 5, 1536, 384], P('site', None, 'sector')
All inputs are finite; a program needn't handle non-finite values.
Results may differ from a plain program's by a relative error of at most 0.0054.
Values may be sent and summed in bfloat16 or wider, within the bound.
A program may use at most 64 MiB of HBM per device.

v0:
```python
import jax
import jax.numpy as jnp
import numpy as np
from jax import lax
from jax.sharding import PartitionSpec as P

W = 5


charge_steps = (0, 1, -1, 0, 0)


def shifted(value, axis, steps):
    count = lax.axis_size(axis)
    first, last = (max(0, -steps), min(count, count - steps))
    return lax.ppermute(value, axis, [(source, source + steps) for source in range(first, last)])


def extended(cells, sides, width):
    for axis, dim in sides:
        count = lax.axis_size(axis)
        head = lax.slice_in_dim(cells, 0, width, axis=dim)
        tail = lax.slice_in_dim(cells, cells.shape[dim] - width, cells.shape[dim], axis=dim)
        cells = jnp.concatenate(
            [
                lax.ppermute(tail, axis, [(i, (i + 1) % count) for i in range(count)]),
                cells,
                lax.ppermute(head, axis, [((i + 1) % count, i) for i in range(count)]),
            ],
            axis=dim,
        )
    return cells


def from_behind(value, axis, steps):
    count = lax.axis_size(axis)
    pairs = [(source, (source + steps) % count) for source in range(count)]
    return lax.ppermute(value, axis, pairs)


def allowed():
    charges = np.array(charge_steps)
    spins = np.arange(2)
    differ = charges[None, :] - charges[:, None]
    return (
        spins[None, None, None, :] - spins[None, None, :, None] == differ[:, :, None, None]
    ).astype(np.float32)


def pick_blocks(near_blocks, sector_width):
    return jnp.stack(
        [
            near_blocks[
                :, (1 + charge_steps[term]) * sector_width : (2 + charge_steps[term]) * sector_width
            ]
            for term in range(W)
        ]
    )


def receive_env(state, boundary, at_start):
    arrived = shifted(state, "site", 1)
    return jnp.where(at_start, boundary, arrived)


def local(site_tensors, environments, mpo, boundary):
    blocks = site_tensors[0]
    sector_width = blocks.shape[2]
    couplings = mpo[0] * allowed()
    near_blocks = extended(blocks, (("sector", 1),), sector_width)
    own_stack = pick_blocks(near_blocks, sector_width)
    at_start = lax.axis_index("site") == 0
    state = environments[0]
    incoming = receive_env(state, boundary, at_start)
    products = jnp.einsum("wab,wtbc->wtac", incoming, own_stack, preferred_element_type=jnp.float32)
    combined = jnp.einsum(
        "wvst,wtac->vsac", couplings, products, precision=lax.Precision.HIGHEST
    ).astype(jnp.bfloat16)
    own_part = jnp.einsum(
        "ba,vbc->vac", blocks[0], combined[:, 0], preferred_element_type=jnp.float32
    )
    carried_part = jnp.einsum(
        "ba,vbc->vac", blocks[1], combined[:, 1], preferred_element_type=jnp.float32
    ).astype(jnp.bfloat16)
    carried = from_behind(carried_part, "sector", 1)
    state = (own_part + carried.astype(jnp.float32)).astype(jnp.bfloat16)
    return state[None]


def solution(mesh):
    in_specs = (
        P("site", None, "sector", None),
        P("site", None, "sector", None),
        P("site", None, None, None, None),
        P(None, "sector", None),
    )
    out_specs = P("site", None, "sector", None)
    return jax.shard_map(local, mesh=mesh, in_specs=in_specs, out_specs=out_specs, check_vma=False)
```

profile of v0, /device:TPU:28, one launch (start us, length us, event | category | flops | bytes accessed | tf_op | source)
XLA Modules:
  0.0 92.4 jit_solution(1129867089160938426)
XLA Ops:
  0.0 0.0 copy-start
  0.0 3.5 %collective-permute-start.2 = (bf16[5,384,384]{2,1,0:T(8,128)(2,1)}, bf16[5,384,384]{2,1,0:T(8,128)(2,1)S(1)}, u32[]{:S(2)}, u32[]{:S(2)}) collective-permute-start(bf16[5,384,384]{2,1,0:T(8,128)(2,1)} %bitcast.52), channel_id=1, source_target_pairs={{0,4},{4,8},{8,12},{12,16},{16,20},{20,24},{24,28},{1,5},{5,9},{9,... | collective-permute-start | bytes 4423688 | tf_op jit(solution)/shard_map/ppermute | solution.py:16
  3.5 0.1 collective-permute-start
  3.6 0.5 collective-permute-start.1
  4.1 0.0 copy-start.1
  4.1 1.2 %constant_dynamic-update-slice_fusion.2 = bf16[5,2,384,384]{3,2,1,0:T(8,128)(2,1)S(1)} fusion(bf16[1,2,384,384]{3,2,1,0:T(8,128)(2,1)} %param.5), kind=kLoop, calls=%fused_computation.25 | loop fusion | bytes 1179648
  5.3 0.7 multiply_bitcast_fusion
  6.1 11.0 %collective-permute-done = bf16[2,384,384]{2,1,0:T(8,128)(2,1)S(1)} collective-permute-done((bf16[2,384,384]{2,1,0:T(8,128)(2,1)}, bf16[2,384,384]{2,1,0:T(8,128)(2,1)S(1)}, u32[]{:S(2)}, u32[]{:S(2)}) %collective-permute-start) | collective-permute-done | bytes 589856 | tf_op jit(solution)/shard_map/ppermute | solution.py:28
  17.1 0.1 bitcast_dynamic-update-slice_fusion.1
  17.2 2.0 %collective-permute-done.1 = bf16[2,384,384]{2,1,0:T(8,128)(2,1)S(1)} collective-permute-done((bf16[2,384,384]{2,1,0:T(8,128)(2,1)}, bf16[2,384,384]{2,1,0:T(8,128)(2,1)S(1)}, u32[]{:S(2)}, u32[]{:S(2)}) %collective-permute-start.1) | collective-permute-done | bytes 589856 | tf_op jit(solution)/shard_map/ppermute | solution.py:26
  19.2 0.1 bitcast_dynamic-update-slice_fusion
  19.3 0.0 copy-done
  19.3 0.1 constant_dynamic-update-slice_fusion.1
  19.4 0.1 constant_dynamic-update-slice_fusion
  19.5 17.7 %collective-permute-done.2 = bf16[5,384,384]{2,1,0:T(8,128)(2,1)S(1)} collective-permute-done((bf16[5,384,384]{2,1,0:T(8,128)(2,1)}, bf16[5,384,384]{2,1,0:T(8,128)(2,1)S(1)}, u32[]{:S(2)}, u32[]{:S(2)}) %collective-permute-start.2) | collective-permute-done | bytes 1474592 | tf_op jit(solution)/shard_map/ppermute | solution.py:16
  37.2 0.0 copy-done.1
  37.2 4.9 %fusion.5 = f32[5,2,384,384]{3,2,1,0:T(8,128)} fusion(bf16[5,2,384,384]{3,2,1,0:T(8,128)(2,1)S(1)} %constant_dynamic-update-slice_fusion, bf16[5,384,384]{2,1,0:T(8,128)(2,1)S(1)} %copy-done.1, bf16[5,384,384]{2,1,0:T(8,128)(2,1)S(1)} %collective-permute-done.2, pred[]{:T(512)S(6)} %eq.3), kind=kOutput, calls=%fused_computation.8 | convolution fusion | flops 1133199360 | bytes 11796481 | tf_op jit(solution)/shard_map/wab,wtbc->wtac/dot_general | solution.py:75
  42.0 8.7 %copy.11 = f32[5,2,384,384]{2,0,1,3:T(8,128)} copy(f32[5,2,384,384]{3,2,1,0:T(8,128)} %fusion.5) | data formatting | bytes 11796480 | tf_op jit(solution)/shard_map/wab,wtbc->wtac/dot_general | solution.py:75
  50.8 17.9 %bitcast_convert_fusion = bf16[5,2,384,384]{3,0,2,1:T(8,128)(2,1)S(1)} fusion(f32[5,2,384,384]{2,0,1,3:T(8,128)} %copy.11, f32[5,5,2,2,1]{1,3,2,0,4:T(2,128)S(1)} %multiply_bitcast_fusion), kind=kOutput, calls=%fused_computation.2 | convolution fusion | flops 178421760 | bytes 8847760 | tf_op jit(solution)/shard_map/wvst,wtac->vsac/dot_general | solution.py:76
  68.7 0.5 slice_bitcast_fusion.1
  69.1 1.1 %fusion.11 = bf16[5,384,384]{1,2,0:T(8,128)(2,1)S(1)} fusion(bf16[5,384,384]{2,0,1:T(8,128)(2,1)S(1)} %get-tuple-element.6, bf16[1,2,384,384]{3,2,1,0:T(8,128)(2,1)S(1)} %copy-done), kind=kOutput, calls=%fused_computation.14 | convolution fusion | flops 566968320 | bytes 4128768 | tf_op jit(solution)/shard_map/ba,vbc->vac/dot_general | solution.py:82
  70.3 0.1 collective-permute-start.3
  70.3 18.8 %collective-permute-done.3 = bf16[5,384,384]{1,2,0:T(8,128)(2,1)S(1)} collective-permute-done((bf16[5,384,384]{1,2,0:T(8,128)(2,1)S(1)}, bf16[5,384,384]{1,2,0:T(8,128)(2,1)S(1)}, u32[]{:S(2)}, u32[]{:S(2)}) %collective-permute-start.3) | collective-permute-done | bytes 1474592 | tf_op jit(solution)/shard_map/ppermute | solution.py:38
  89.1 1.1 %fusion.14 = bf16[1,5,384,384]{2,3,1,0:T(8,128)(2,1)S(1)} fusion(bf16[5,384,384]{1,2,0:T(8,128)(2,1)S(1)} %collective-permute-done.3, bf16[5,384,384]{2,0,1:T(8,128)(2,1)S(1)} %get-tuple-element.5, bf16[1,2,384,384]{3,2,1,0:T(8,128)(2,1)S(1)} %copy-done), kind=kOutput, calls=%fused_computation.15 | convolution fusion | flops 568442880 | bytes 5603328 | tf_op jit(solution)/shard_map/ba,vbc->vac/dot_general | solution.py:79
  90.3 2.2 %copy.9 = bf16[1,5,384,384]{3,2,1,0:T(8,128)(2,1)} copy(bf16[1,5,384,384]{2,3,1,0:T(8,128)(2,1)S(1)} %fusion.14) | data formatting | bytes 2949120 | tf_op jit(solution)/shard_map/broadcast_in_dim | solution.py:87
Async XLA Ops:
  0.0 19.3 %copy-start = (bf16[1,2,384,384]{3,2,1,0:T(8,128)(2,1)S(1)}, bf16[1,2,384,384]{3,2,1,0:T(8,128)(2,1)}, u32[]{:S(2)}) copy-start(bf16[1,2,384,384]{3,2,1,0:T(8,128)(2,1)} %param.5) | copy-start | bytes 1769476
  0.0 37.1 %collective-permute-start.2 = (bf16[5,384,384]{2,1,0:T(8,128)(2,1)}, bf16[5,384,384]{2,1,0:T(8,128)(2,1)S(1)}, u32[]{:S(2)}, u32[]{:S(2)}) collective-permute-start(bf16[5,384,384]{2,1,0:T(8,128)(2,1)} %bitcast.52), channel_id=1, source_target_pairs={{0,4},{4,8},{8,12},{12,16},{16,20},{20,24},{24,28},{1,5},{5,9},{9,... | collective-permute-start | bytes 4423688 | tf_op jit(solution)/shard_map/ppermute | solution.py:16
  3.5 13.5 %collective-permute-start = (bf16[2,384,384]{2,1,0:T(8,128)(2,1)}, bf16[2,384,384]{2,1,0:T(8,128)(2,1)S(1)}, u32[]{:S(2)}, u32[]{:S(2)}) collective-permute-start(bf16[2,384,384]{2,1,0:T(8,128)(2,1)} %bitcast.50), channel_id=1, source_target_pairs={{1,0},{2,1},{3,2},{0,3},{5,4},{6,5},{7,6},{4,7},{9,8},{10,9},{11,1... | collective-permute-start | bytes 1769480 | tf_op jit(solution)/shard_map/ppermute | solution.py:28
  3.6 15.6 %collective-permute-start.1 = (bf16[2,384,384]{2,1,0:T(8,128)(2,1)}, bf16[2,384,384]{2,1,0:T(8,128)(2,1)S(1)}, u32[]{:S(2)}, u32[]{:S(2)}) collective-permute-start(bf16[2,384,384]{2,1,0:T(8,128)(2,1)} %bitcast.51), channel_id=1, source_target_pairs={{0,1},{1,2},{2,3},{3,0},{4,5},{5,6},{6,7},{7,4},{8,9},{9,10},{10,1... | collective-permute-start | bytes 1769480 | tf_op jit(solution)/shard_map/ppermute | solution.py:26
  4.1 33.1 %copy-start.1 = (bf16[5,384,384]{2,1,0:T(8,128)(2,1)S(1)}, bf16[5,384,384]{2,1,0:T(8,128)(2,1)}, u32[]{:S(2)}) copy-start(bf16[5,384,384]{2,1,0:T(8,128)(2,1)} %param.8) | copy-start | bytes 4423684
  70.3 18.8 %collective-permute-start.3 = (bf16[5,384,384]{1,2,0:T(8,128)(2,1)S(1)}, bf16[5,384,384]{1,2,0:T(8,128)(2,1)S(1)}, u32[]{:S(2)}, u32[]{:S(2)}) collective-permute-start(bf16[5,384,384]{1,2,0:T(8,128)(2,1)S(1)} %fusion.11), channel_id=1, source_target_pairs={{0,1},{1,2},{2,3},{3,0},{4,5},{5,6},{6,7},{7,4},{8,9},{9,10},{10,1... | collective-permute-start | bytes 4423688 | tf_op jit(solution)/shard_map/ppermute | solution.py:38
where the time goes:
time: 92.8 us; the launch traced here: 92.4 us
  waiting for transfers between devices  49.4 us (53%)
  matrix products  25 us (27%)
  local copies, waits for them, and re-layouts  13 us (14%)
  starting transfers between devices  4.13 us (4%)
    ppermute x1, waiting for transfers between devices, from_behind(): return lax.ppermute(value, axis, pairs)  18.8 us
    dot_general x1, matrix products, local(): jnp.einsum('wvst,wtac->vsac', couplings, products, precision=lax.Precisio...  17.9 us
    ppermute x1, waiting for transfers between devices, shifted(): lax.ppermute(value, axis, [(source, source + steps) for source in range(f...  17.7 us
    ppermute x1, waiting for transfers between devices, extended(): lax.ppermute(head, axis, [((i + 1) % count, i) for i in range(count)])  11 us
    dot_general x1, local copies, waits for them, and re-layouts, local(): jnp.einsum('wab,wtbc->wtac', incoming, own_stack, preferred_element_type=...  8.72 us
    dot_general x1, matrix products, local(): jnp.einsum('wab,wtbc->wtac', incoming, own_stack, preferred_element_type=...  4.88 us
    ppermute x1, starting transfers between devices, shifted(): lax.ppermute(value, axis, [(source, source + steps) for source in range(f...  3.52 us
    broadcast_in_dim x1, local copies, waits for them, and re-layouts, local(): return state[None]  2.16 us
  transfers between devices with their start and end apart: 4, of which 4 were waited for; matrix products, arithmetic and copies ran while one was open for 3% of the time, Pallas kernels for 0%

commit v1 on v0

v1 whole, which is shorter than its diff:
```python
import functools

import jax
import jax.numpy as jnp
from jax import lax
from jax.experimental import pallas as pl
from jax.experimental.pallas import tpu as pltpu
from jax.sharding import PartitionSpec as P

MESH = pl.DeviceIdType.MESH
charge_steps = (0, 1, -1, 0, 0)
W = len(charge_steps)
ORDER = (1, 0, 3, 4, 2)
DEPTH = 2


def targets(w, t):
    return [
        (v, s)
        for v in range(W)
        for s in range(2)
        if t - s == charge_steps[v] - charge_steps[w]
    ]


def dot(a, b):
    return jnp.dot(a, b, preferred_element_type=jnp.float32)


def kernel(
    ns, nq, site, env, mpo, bnd, out,
    inc, near, flip, total, carry_out, carry_in,
    env_send, env_recv, near_send, near_recv, carry_send, carry_recv, local_sem,
):
    s = lax.axis_index("site")
    q = lax.axis_index("sector")
    nxt, prv = lax.rem(s + 1, ns), lax.rem(s + ns - 1, ns)
    above, below = lax.rem(q + 1, nq), lax.rem(q + nq - 1, nq)
    has_next, has_prev = s < ns - 1, s > 0

    barrier = pltpu.get_barrier_semaphore()
    for other in (above, below):
        pl.semaphore_signal(barrier, inc=1, device_id={"site": s, "sector": other}, device_id_type=MESH)

    @pl.when(has_next)
    def _():
        pl.semaphore_signal(barrier, inc=1, device_id={"site": nxt, "sector": q}, device_id_type=MESH)

    @pl.when(has_prev)
    def _():
        pl.semaphore_signal(barrier, inc=1, device_id={"site": prv, "sector": q}, device_id_type=MESH)

    pl.semaphore_wait(barrier, 2 + has_next.astype(jnp.int32) + has_prev.astype(jnp.int32))

    def env_copy(k):
        w = ORDER[k]
        return pltpu.make_async_remote_copy(
            src_ref=env.at[0, w], dst_ref=inc.at[w],
            send_sem=env_send.at[k], recv_sem=env_recv.at[k],
            device_id={"site": nxt, "sector": q}, device_id_type=MESH,
        )

    def start_env(k):
        @pl.when(has_next)
        def _():
            env_copy(k).start()

    near_copies = [
        pltpu.make_async_remote_copy(
            src_ref=site.at[0], dst_ref=near.at[i],
            send_sem=near_send.at[i], recv_sem=near_recv.at[i],
            device_id={"site": s, "sector": other}, device_id_type=MESH,
        )
        for i, other in ((0, above), (1, below))
    ]
    carry_copies = [
        pltpu.make_async_remote_copy(
            src_ref=carry_out.at[v], dst_ref=carry_in.at[v],
            send_sem=carry_send.at[v], recv_sem=carry_recv.at[v],
            device_id={"site": s, "sector": above}, device_id_type=MESH,
        )
        for v in range(W)
    ]

    for k in range(DEPTH):
        start_env(k)
    near_copies[1].start()
    near_copies[0].start()

    @pl.when(jnp.logical_not(has_prev))
    def _():
        copy = pltpu.make_async_copy(bnd, inc, local_sem)
        copy.start()
        copy.wait()

    for t in range(2):
        flip[t] = site[0, t].T

    left = {(v, x): sum((v, x) in targets(w, t) for w in range(W) for t in range(2)) for v in range(W) for x in range(2)}
    begun, seen = set(), set()
    for k, w in enumerate(ORDER):
        if k + DEPTH <= W - 1:
            @pl.when(has_next)
            def _():
                env_copy(k).wait_send()
                env_copy(k + DEPTH).start()

        @pl.when(has_prev)
        def _():
            env_copy(k).wait_recv()

        step = charge_steps[w]
        if step and step not in seen:
            near_copies[(step + 1) // 2].wait_recv()
            seen.add(step)
        done = []
        for t in (1, 0):
            block = site[0, t] if step == 0 else near[(step + 1) // 2, t]
            product = dot(inc[w], block)
            for v, x in targets(w, t):
                term = mpo[0, w, v, x, t] * product
                if (v, x) in begun:
                    total[v, x] += term
                else:
                    total[v, x] = term
                    begun.add((v, x))
                left[v, x] -= 1
                if not left[v, x]:
                    done.append((v, x))
        for v, x in sorted(done, key=lambda item: -item[1]):
            part = dot(flip[x], total[v, x].astype(jnp.bfloat16))
            if x:
                carry_out[v] = part.astype(jnp.bfloat16)
                carry_copies[v].start()
            else:
                total[v, 0] = part

    for v in (1, 0, 3, 4, 2):
        carry_copies[v].wait_recv()
        out[0, v] = (total[v, 0] + carry_in[v].astype(jnp.float32)).astype(jnp.bfloat16)

    for copy in near_copies + carry_copies:
        copy.wait_send()

    @pl.when(has_next)
    def _():
        for k in range(W - DEPTH, W):
            env_copy(k).wait_send()


def solution(mesh):
    ns, nq = mesh.shape["site"], mesh.shape["sector"]

    def local(site_tensors, environments, mpo, boundary):
        width = site_tensors.shape[3]
        vmem = functools.partial(pltpu.VMEM)
        dma = pltpu.SemaphoreType.DMA
        bf16, f32 = jnp.bfloat16, jnp.float32
        return pl.pallas_call(
            functools.partial(kernel, ns, nq),
            out_shape=jax.ShapeDtypeStruct(environments.shape, bf16),
            in_specs=[
                pl.BlockSpec(memory_space=pltpu.VMEM),
                pl.BlockSpec(memory_space=pl.ANY),
                pl.BlockSpec(memory_space=pltpu.SMEM),
                pl.BlockSpec(memory_space=pl.ANY),
            ],
            out_specs=pl.BlockSpec(memory_space=pltpu.VMEM),
            scratch_shapes=[
                vmem((W, width, width), bf16),
                vmem((2, 2, width, width), bf16),
                vmem((2, width, width), bf16),
                vmem((W, 2, width, width), f32),
                vmem((W, width, width), bf16),
                vmem((W, width, width), bf16),
                dma((W,)), dma((W,)), dma((2,)), dma((2,)), dma((W,)), dma((W,)), dma,
            ],
            compiler_params=pltpu.CompilerParams(
                collective_id=0, has_side_effects=True, vmem_limit_bytes=48 * 2**20
            ),
            cost_estimate=pl.CostEstimate(
                flops=40 * width**3, bytes_accessed=24 * W * width * width, transcendentals=0
            ),
        )(site_tensors, environments, mpo, boundary)

    return jax.shard_map(
        local,
        mesh=mesh,
        in_specs=(
            P("site", None, "sector", None),
            P("site", None, "sector", None),
            P("site", None, None, None, None),
            P(None, "sector", None),
        ),
        out_specs=P("site", None, "sector", None),
        check_vma=False,
    )
```

time: 92.8 us -> 50.9 us (0.55)
  waiting for transfers between devices: 49.4 us -> 0 us
  Pallas kernels: 0 us -> 44.8 us
  matrix products: 25 us -> 0 us
  local copies, waits for them, and re-layouts: 13 us -> 5.76 us
  starting transfers between devices: 4.13 us -> 0 us
    ppermute x4 -> x0, waiting for transfers between devices: 49.4 us -> none  [the longest x1 18.8 us: from_behind(): return lax.ppermute(value, axis, pairs)]
    pallas_call x0 -> x1, Pallas kernels: none -> 44.8 us  [local(): pl.pallas_call(functools.partial(kernel, ns, nq), out_shape=jax.ShapeDtyp...]
    dot_general x4 -> x0, matrix products: 25 us -> none  [the longest x1 17.9 us: local(): jnp.einsum('wvst,wtac->vsac', couplings, products, precision=lax.Precisio...]
    dot_general x1 -> x0, local copies, waits for them, and re-layouts: 8.72 us -> none  [local(): jnp.einsum('wab,wtbc->wtac', incoming, own_stack, preferred_element_type=...]
    unnamed x8, local copies, waits for them, and re-layouts: 1.54 us -> 5.76 us
    ppermute x4 -> x0, starting transfers between devices: 4.13 us -> none  [the longest x1 3.52 us: shifted(): lax.ppermute(value, axis, [(source, source + steps) for source in range(f...]
    broadcast_in_dim x1 -> x0, local copies, waits for them, and re-layouts: 2.16 us -> none  [local(): return state[None]]
  transfers between devices with their start and end apart: 4 -> 0, of which waited for: 4 -> 0; matrix products, arithmetic and copies ran while one was open for 3% -> 0% of each run, Pallas kernels for 0% -> 0%
where the time goes in v1:
time: 50.9 us; the launch traced here: 50.6 us
  Pallas kernels  44.8 us (88%)
  local copies, waits for them, and re-layouts  5.76 us (11%)
    pallas_call x1, Pallas kernels, local(): pl.pallas_call(functools.partial(kernel, ns, nq), out_shape=jax.ShapeDtyp...  44.8 us
    unnamed x8, local copies, waits for them, and re-layouts  5.76 us

profile of v1, /device:TPU:28, one launch (start us, length us, event | category | flops | bytes accessed | tf_op | source)
XLA Modules:
  0.0 50.6 jit_solution(11641784269654962232)
XLA Ops:
  0.0 0.8 %copy.5.mpo = f32[1,5,5,2,2]{4,3,2,1,0:T(2,128)S(1)} copy(f32[1,5,5,2,2]{2,4,3,1,0:T(2,128)} %param.6) | data formatting | bytes 800 | tf_op args[2]
  0.8 0.0 copy-start
  0.8 1.4 %copy-done = bf16[1,5,384,384]{3,2,1,0:T(8,128)(2,1)S(1)} copy-done((bf16[1,5,384,384]{3,2,1,0:T(8,128)(2,1)S(1)}, bf16[1,5,384,384]{3,2,1,0:T(8,128)(2,1)}, u32[]{:S(2)}) %copy-start) | copy-done | bytes 1474584
  2.2 0.0 copy-start.1
  2.2 1.4 %copy-done.1 = bf16[5,384,384]{2,1,0:T(8,128)(2,1)S(1)} copy-done((bf16[5,384,384]{2,1,0:T(8,128)(2,1)S(1)}, bf16[5,384,384]{2,1,0:T(8,128)(2,1)}, u32[]{:S(2)}) %copy-start.1) | copy-done | bytes 1474584
  3.6 0.0 copy-start.2
  3.6 1.1 %copy-done.2 = bf16[1,2,384,384]{3,2,1,0:T(8,128)(2,1)S(1)} copy-done((bf16[1,2,384,384]{3,2,1,0:T(8,128)(2,1)S(1)}, bf16[1,2,384,384]{3,2,1,0:T(8,128)(2,1)}, u32[]{:S(2)}) %copy-start.2) | copy-done | bytes 589848
  4.7 44.8 %shard_map.46 = bf16[1,5,384,384]{3,2,1,0:T(8,128)(2,1)S(1)} custom-call(bf16[1,2,384,384]{3,2,1,0:T(8,128)(2,1)S(1)} %copy-done.2, bf16[1,5,384,384]{3,2,1,0:T(8,128)(2,1)S(1)} %copy-done, f32[1,5,5,2,2]{4,3,2,1,0:T(2,128)S(1)} %copy.5.mpo, bf16[5,384,384]{2,1,0:T(8,128)(2,1)S(1)} %copy-done.1), custom_call_target="tpu_custom_call" | custom-call | flops 2264924160 | bytes 17694720 | tf_op jit(solution)/shard_map/pallas_call | solution.py:159
  49.5 1.1 %copy.7 = bf16[1,5,384,384]{3,2,1,0:T(8,128)(2,1)} copy(bf16[1,5,384,384]{3,2,1,0:T(8,128)(2,1)S(1)} %shard_map.46) | data formatting | bytes 2949120
Async XLA Ops:
  0.8 1.4 %copy-start = (bf16[1,5,384,384]{3,2,1,0:T(8,128)(2,1)S(1)}, bf16[1,5,384,384]{3,2,1,0:T(8,128)(2,1)}, u32[]{:S(2)}) copy-start(bf16[1,5,384,384]{3,2,1,0:T(8,128)(2,1)} %env.1) | copy-start | bytes 4423684
  2.2 1.4 %copy-start.1 = (bf16[5,384,384]{2,1,0:T(8,128)(2,1)S(1)}, bf16[5,384,384]{2,1,0:T(8,128)(2,1)}, u32[]{:S(2)}) copy-start(bf16[5,384,384]{2,1,0:T(8,128)(2,1)} %bnd.1) | copy-start | bytes 4423684
  3.6 1.1 %copy-start.2 = (bf16[1,2,384,384]{3,2,1,0:T(8,128)(2,1)S(1)}, bf16[1,2,384,384]{3,2,1,0:T(8,128)(2,1)}, u32[]{:S(2)}) copy-start(bf16[1,2,384,384]{3,2,1,0:T(8,128)(2,1)} %site.1) | copy-start | bytes 1769476

commit v2 on v1

v2 whole, which is shorter than its diff:
```python
import functools

import jax
import jax.numpy as jnp
from jax import lax
from jax.experimental import pallas as pl
from jax.experimental.pallas import tpu as pltpu
from jax.sharding import PartitionSpec as P

MESH = pl.DeviceIdType.MESH
charge_steps = (0, 1, -1, 0, 0)
W = len(charge_steps)
ORDER = (1, 2, 0, 3, 4)
DEPTH = 2


def uses(w, t, x):
    return [v for v in range(W) if t - x == charge_steps[v] - charge_steps[w]]


def dot(a, b):
    return jnp.dot(a, b, preferred_element_type=jnp.float32)


def chunks_of(width):
    whole = [(w, 0, width) for w in ORDER[:-1]]
    cut = width - max(width // 3, 16)
    return whole + [(ORDER[-1], 0, cut), (ORDER[-1], cut, width - cut)]


def kernel(
    ns, nq, site_hbm, env, mpo, bnd, out,
    site, inc, low, below_site, above_site, flip, total, part, pair_out,
    env_send, env_recv, relay_send, relay_recv, near_send, near_recv, local_sem,
):
    s = lax.axis_index("site")
    q = lax.axis_index("sector")
    nxt, prv = lax.rem(s + 1, ns), lax.rem(s + ns - 1, ns)
    above, below = lax.rem(q + 1, nq), lax.rem(q + nq - 1, nq)
    has_next, has_prev = s < ns - 1, s > 0
    width = site.shape[-1]
    chunks = chunks_of(width)
    count = len(chunks)

    def at(place, sector):
        return {"site": place, "sector": sector}

    own_copy = pltpu.make_async_copy(site_hbm.at[0], site, local_sem.at[0])
    own_copy.start()
    bnd_copy = pltpu.make_async_copy(bnd, inc, local_sem.at[1])

    @pl.when(jnp.logical_not(has_prev))
    def _():
        bnd_copy.start()

    barrier = pltpu.get_barrier_semaphore()
    for other in (above, below):
        pl.semaphore_signal(barrier, inc=1, device_id=at(s, other), device_id_type=MESH)

    @pl.when(has_next)
    def _():
        pl.semaphore_signal(barrier, inc=1, device_id=at(nxt, q), device_id_type=MESH)

    @pl.when(has_prev)
    def _():
        pl.semaphore_signal(barrier, inc=1, device_id=at(prv, q), device_id_type=MESH)

    pl.semaphore_wait(barrier, 2 + has_next.astype(jnp.int32) + has_prev.astype(jnp.int32))

    def env_copy(k):
        w, row, rows = chunks[k]
        return pltpu.make_async_remote_copy(
            src_ref=env.at[0, w, pl.ds(row, rows)], dst_ref=inc.at[w, pl.ds(row, rows)],
            send_sem=env_send.at[k], recv_sem=env_recv.at[k],
            device_id=at(nxt, q), device_id_type=MESH,
        )

    def relay_copy(k):
        w, row, rows = chunks[k]
        source = pair_out if charge_steps[w] < 0 else inc.at[w, pl.ds(row, rows)]
        return pltpu.make_async_remote_copy(
            src_ref=source, dst_ref=low.at[w, pl.ds(row, rows)],
            send_sem=relay_send.at[k], recv_sem=relay_recv.at[k],
            device_id=at(s, above), device_id_type=MESH,
        )

    to_below = pltpu.make_async_remote_copy(
        src_ref=site_hbm.at[0, 0], dst_ref=above_site,
        send_sem=near_send.at[0], recv_sem=near_recv.at[0],
        device_id=at(s, below), device_id_type=MESH,
    )
    to_above = pltpu.make_async_remote_copy(
        src_ref=site_hbm.at[0], dst_ref=below_site,
        send_sem=near_send.at[1], recv_sem=near_recv.at[1],
        device_id=at(s, above), device_id_type=MESH,
    )

    @pl.when(has_next)
    def _():
        for k in range(DEPTH):
            env_copy(k).start()

    to_below.start()
    to_above.start()

    own_copy.wait()
    flip[0] = site[0].T

    @pl.when(jnp.logical_not(has_prev))
    def _():
        bnd_copy.wait()

    begun = set()
    left = {
        (v, x): sum(v in uses(w, t, x) for w in range(W) for t in range(2))
        for v in range(W) for x in range(2)
    }

    def add(product, k, t, x):
        w, row, rows = chunks[k]
        final = row + rows == width
        for v in uses(w, t, x):
            term = mpo[0, w, x, t, v] * product
            last = left[v, x] == 1
            if final:
                left[v, x] -= 1
            if (v, x) in begun:
                term = total[v, x, row:row + rows] + term
            if last:
                piece = dot(flip[x, :, row:row + rows], term.astype(jnp.bfloat16))
                if row:
                    piece = part[v, x] + piece
                if x and w == ORDER[-1] and final:
                    carried = piece.astype(jnp.bfloat16).astype(jnp.float32)
                    out[0, v] = (part[v, 0] + carried).astype(jnp.bfloat16)
                else:
                    part[v, x] = piece
            else:
                total[v, x, row:row + rows] = term
                if final:
                    begun.add((v, x))

    def own(k):
        w, row, rows = chunks[k]
        step = charge_steps[w]
        rows_in = inc[w, row:row + rows]
        for t in (1, 0):
            if not uses(w, t, 0) and not (step < 0 and t == 1):
                continue
            block = site[t] if step == 0 else above_site[...] if step > 0 else below_site[t]
            product = dot(rows_in, block)
            if step < 0 and t == 1:
                pair_out[...] = product.astype(jnp.bfloat16)
                relay_copy(k).start()
            add(product, k, t, 0)

    def lower(k):
        w, row, rows = chunks[k]
        step = charge_steps[w]
        relay_copy(k).wait_recv()
        rows_in = low[w, row:row + rows]
        if step < 0:
            add(rows_in.astype(jnp.float32), k, 1, 1)
            return
        for t in (1, 0):
            if uses(w, t, 1):
                add(dot(rows_in, below_site[t] if step == 0 else site[t]), k, t, 1)

    for k, (w, row, rows) in enumerate(chunks):
        @pl.when(has_prev)
        def _():
            env_copy(k).wait_recv()

        if charge_steps[w] >= 0:
            relay_copy(k).start()

        if k + DEPTH < count:
            @pl.when(has_next)
            def _():
                env_copy(k).wait_send()
                env_copy(k + DEPTH).start()

        if k == 0:
            to_below.wait_recv()
            to_above.wait_recv()
            flip[1] = below_site[1].T
        own(k)
        if k:
            lower(k - 1)
    carried = part[1, 1].astype(jnp.bfloat16).astype(jnp.float32)
    out[0, 1] = (part[1, 0] + carried).astype(jnp.bfloat16)
    lower(count - 1)

    to_below.wait_send()
    to_above.wait_send()
    for k in range(count):
        relay_copy(k).wait_send()

    @pl.when(has_next)
    def _():
        for k in range(count - DEPTH, count):
            env_copy(k).wait_send()


def solution(mesh):
    ns, nq = mesh.shape["site"], mesh.shape["sector"]

    def local(site_tensors, environments, mpo, boundary):
        width = site_tensors.shape[3]
        count = len(chunks_of(width))
        vmem, dma = pltpu.VMEM, pltpu.SemaphoreType.DMA
        bf16, f32 = jnp.bfloat16, jnp.float32
        return pl.pallas_call(
            functools.partial(kernel, ns, nq),
            out_shape=jax.ShapeDtypeStruct(environments.shape, bf16),
            in_specs=[
                pl.BlockSpec(memory_space=pltpu.HBM),
                pl.BlockSpec(memory_space=pltpu.HBM),
                pl.BlockSpec(memory_space=pltpu.SMEM),
                pl.BlockSpec(memory_space=pltpu.HBM),
            ],
            out_specs=pl.BlockSpec(memory_space=pltpu.VMEM),
            scratch_shapes=[
                vmem((2, width, width), bf16),
                vmem((W, width, width), bf16),
                vmem((W, width, width), bf16),
                vmem((2, width, width), bf16),
                vmem((width, width), bf16),
                vmem((2, width, width), bf16),
                vmem((W, 2, width, width), f32),
                vmem((W, 2, width, width), f32),
                vmem((width, width), bf16),
                dma((count,)), dma((count,)), dma((count,)), dma((count,)),
                dma((2,)), dma((2,)), dma((2,)),
            ],
            compiler_params=pltpu.CompilerParams(
                collective_id=0, has_side_effects=True, vmem_limit_bytes=60 * 2**20
            ),
            cost_estimate=pl.CostEstimate(
                flops=54 * width**3, bytes_accessed=24 * W * width * width, transcendentals=0
            ),
        )(site_tensors, environments, mpo.transpose(0, 1, 3, 4, 2), boundary)

    return jax.shard_map(
        local,
        mesh=mesh,
        in_specs=(
            P("site", None, "sector", None),
            P("site", None, "sector", None),
            P("site", None, None, None, None),
            P(None, "sector", None),
        ),
        out_specs=P("site", None, "sector", None),
        check_vma=False,
    )
```

time: 50.9 us -> 43.7 us (0.86)
  Pallas kernels: 44.8 us -> 40.8 us
  local copies, waits for them, and re-layouts: 5.76 us -> 2.63 us
    pallas_call x1, Pallas kernels: 44.8 us -> 40.8 us  [local(): pl.pallas_call(functools.partial(kernel, ns, nq), out_shape=jax.ShapeDtyp...]
    unnamed x8 -> x1, local copies, waits for them, and re-layouts: 5.76 us -> 2.63 us
where the time goes in v2:
time: 43.7 us; the launch traced here: 43.5 us
  Pallas kernels  40.8 us (93%)
  local copies, waits for them, and re-layouts  2.63 us (6%)
    pallas_call x1, Pallas kernels, local(): pl.pallas_call(functools.partial(kernel, ns, nq), out_shape=jax.ShapeDtyp...  40.8 us
    unnamed x1, local copies, waits for them, and re-layouts  2.63 us

profile of v2, /device:TPU:28, one launch (start us, length us, event | category | flops | bytes accessed | tf_op | source)
XLA Modules:
  0.0 43.5 jit_solution(2187816294404329726)
XLA Ops:
  0.0 40.8 %shard_map.46 = bf16[1,5,384,384]{3,2,1,0:T(8,128)(2,1)} custom-call(bf16[1,2,384,384]{3,2,1,0:T(8,128)(2,1)} %site_hbm.1, bf16[1,5,384,384]{3,2,1,0:T(8,128)(2,1)} %env.1, f32[1,5,2,2,5]{4,3,2,1,0:T(2,128)} %bitcast.1, bf16[5,384,384]{2,1,0:T(8,128)(2,1)} %bnd.1), custom_call_target="tpu_custom_call" | custom-call | flops 3057647616 | bytes 17694720 | tf_op jit(solution)/shard_map/pallas_call | solution.py:213
  40.8 2.6 %copy.6 = bf16[1,5,384,384]{3,2,1,0:T(8,128)(2,1)} copy(bf16[1,5,384,384]{3,2,1,0:T(8,128)(2,1)} %shard_map.46) | data formatting | bytes 2949120

commit v3 on v2

--- a/solution.py
+++ b/solution.py
@@ -11,7 +11,7 @@
 charge_steps = (0, 1, -1, 0, 0)
 W = len(charge_steps)
 ORDER = (1, 2, 0, 3, 4)
-DEPTH = 2
+DEPTH = 3
 
 
 def uses(w, t, x):
@@ -23,9 +23,8 @@
 
 
 def chunks_of(width):
-    whole = [(w, 0, width) for w in ORDER[:-1]]
-    cut = width - max(width // 3, 16)
-    return whole + [(ORDER[-1], 0, cut), (ORDER[-1], cut, width - cut)]
+    cut = width - width // 3
+    return [(w, 0, cut) for w in ORDER] + [(w, cut, width - cut) for w in ORDER]
 
 
 def kernel(
@@ -77,7 +76,7 @@
 
     def relay_copy(k):
         w, row, rows = chunks[k]
-        source = pair_out if charge_steps[w] < 0 else inc.at[w, pl.ds(row, rows)]
+        source = (pair_out if charge_steps[w] < 0 else inc.at[w]).at[pl.ds(row, rows)]
         return pltpu.make_async_remote_copy(
             src_ref=source, dst_ref=low.at[w, pl.ds(row, rows)],
             send_sem=relay_send.at[k], recv_sem=relay_recv.at[k],
@@ -110,35 +109,34 @@
     def _():
         bnd_copy.wait()
 
-    begun = set()
-    left = {
+    seen, complete = {}, set()
+    needed = {
         (v, x): sum(v in uses(w, t, x) for w in range(W) for t in range(2))
         for v in range(W) for x in range(2)
     }
 
     def add(product, k, t, x):
         w, row, rows = chunks[k]
-        final = row + rows == width
         for v in uses(w, t, x):
             term = mpo[0, w, x, t, v] * product
-            last = left[v, x] == 1
-            if final:
-                left[v, x] -= 1
-            if (v, x) in begun:
+            so_far = seen.get((v, x, row), 0)
+            seen[v, x, row] = so_far + 1
+            if so_far:
                 term = total[v, x, row:row + rows] + term
-            if last:
-                piece = dot(flip[x, :, row:row + rows], term.astype(jnp.bfloat16))
-                if row:
-                    piece = part[v, x] + piece
-                if x and w == ORDER[-1] and final:
-                    carried = piece.astype(jnp.bfloat16).astype(jnp.float32)
-                    out[0, v] = (part[v, 0] + carried).astype(jnp.bfloat16)
-                else:
-                    part[v, x] = piece
-            else:
+            if so_far + 1 < needed[v, x]:
                 total[v, x, row:row + rows] = term
-                if final:
-                    begun.add((v, x))
+                continue
+            piece = dot(flip[x, :, row:row + rows], term.astype(jnp.bfloat16))
+            if row:
+                piece = part[v, x] + piece
+            if row and v in complete:
+                own_piece, carried = (part[v, 0], piece) if x else (piece, part[v, 1])
+                carried = carried.astype(jnp.bfloat16).astype(jnp.float32)
+                out[0, v] = (own_piece + carried).astype(jnp.bfloat16)
+                continue
+            part[v, x] = piece
+            if row:
+                complete.add(v)
 
     def own(k):
         w, row, rows = chunks[k]
@@ -150,7 +148,7 @@
             block = site[t] if step == 0 else above_site[...] if step > 0 else below_site[t]
             product = dot(rows_in, block)
             if step < 0 and t == 1:
-                pair_out[...] = product.astype(jnp.bfloat16)
+                pair_out[row:row + rows] = product.astype(jnp.bfloat16)
                 relay_copy(k).start()
             add(product, k, t, 0)
 
@@ -187,8 +185,6 @@
         own(k)
         if k:
             lower(k - 1)
-    carried = part[1, 1].astype(jnp.bfloat16).astype(jnp.float32)
-    out[0, 1] = (part[1, 0] + carried).astype(jnp.bfloat16)
     lower(count - 1)
 
     to_below.wait_send()
@@ -212,7 +208,7 @@
         bf16, f32 = jnp.bfloat16, jnp.float32
         return pl.pallas_call(
             functools.partial(kernel, ns, nq),
-            out_shape=jax.ShapeDtypeStruct(environments.shape, bf16),
+            out_shape=pltpu.VMEM(environments.shape, bf16),
             in_specs=[
                 pl.BlockSpec(memory_space=pltpu.HBM),
                 pl.BlockSpec(memory_space=pltpu.HBM),

time: 43.7 us -> 41 us (0.938)
  local copies, waits for them, and re-layouts: 2.63 us -> 1.11 us
  Pallas kernels: 40.8 us -> 39.7 us
    unnamed x1, local copies, waits for them, and re-layouts: 2.63 us -> 1.11 us
    pallas_call x1, Pallas kernels: 40.8 us -> 39.7 us  [local(): pl.pallas_call(functools.partial(kernel, ns, nq), out_shape=pltpu.VMEM(en...]
where the time goes in v3:
time: 41 us; the launch traced here: 40.8 us
  Pallas kernels  39.7 us (97%)
  local copies, waits for them, and re-layouts  1.11 us (3%)
    pallas_call x1, Pallas kernels, local(): pl.pallas_call(functools.partial(kernel, ns, nq), out_shape=pltpu.VMEM(en...  39.7 us
    unnamed x1, local copies, waits for them, and re-layouts  1.11 us

profile of v3, /device:TPU:28, one launch (start us, length us, event | category | flops | bytes accessed | tf_op | source)
XLA Modules:
  0.0 40.8 jit_solution(11282801643926583932)
XLA Ops:
  0.0 39.7 %shard_map.46 = bf16[1,5,384,384]{3,2,1,0:T(8,128)(2,1)S(1)} custom-call(bf16[1,2,384,384]{3,2,1,0:T(8,128)(2,1)} %site_hbm.1, bf16[1,5,384,384]{3,2,1,0:T(8,128)(2,1)} %env.1, f32[1,5,2,2,5]{4,3,2,1,0:T(2,128)} %bitcast.1, bf16[5,384,384]{2,1,0:T(8,128)(2,1)} %bnd.1), custom_call_target="tpu_custom_call" | custom-call | flops 3057647616 | bytes 17694720 | tf_op jit(solution)/shard_map/pallas_call | solution.py:209
  39.7 1.1 %copy.6 = bf16[1,5,384,384]{3,2,1,0:T(8,128)(2,1)} copy(bf16[1,5,384,384]{3,2,1,0:T(8,128)(2,1)S(1)} %shard_map.46) | data formatting | bytes 2949120

commit v4 on v3

--- a/solution.py
+++ b/solution.py
@@ -10,7 +10,7 @@
 MESH = pl.DeviceIdType.MESH
 charge_steps = (0, 1, -1, 0, 0)
 W = len(charge_steps)
-ORDER = (1, 2, 0, 3, 4)
+ORDER = (1, 0, 3, 4, 2)
 DEPTH = 3
 
 

time: 41 us -> 40.7 us (level)
  no operation moved by 1% of the time
where the time goes in v4:
time: 40.7 us; the launch traced here: 40.5 us
  Pallas kernels  39.4 us (97%)
  local copies, waits for them, and re-layouts  1.11 us (3%)
    pallas_call x1, Pallas kernels, local(): pl.pallas_call(functools.partial(kernel, ns, nq), out_shape=pltpu.VMEM(en...  39.4 us
    unnamed x1, local copies, waits for them, and re-layouts  1.11 us

profile of v4, /device:TPU:28, one launch (start us, length us, event | category | flops | bytes accessed | tf_op | source)
XLA Modules:
  0.0 40.5 jit_solution(12787504128971200207)
XLA Ops:
  0.0 39.4 %shard_map.46 = bf16[1,5,384,384]{3,2,1,0:T(8,128)(2,1)S(1)} custom-call(bf16[1,2,384,384]{3,2,1,0:T(8,128)(2,1)} %site_hbm.1, bf16[1,5,384,384]{3,2,1,0:T(8,128)(2,1)} %env.1, f32[1,5,2,2,5]{4,3,2,1,0:T(2,128)} %bitcast.1, bf16[5,384,384]{2,1,0:T(8,128)(2,1)} %bnd.1), custom_call_target="tpu_custom_call" | custom-call | flops 3057647616 | bytes 17694720 | tf_op jit(solution)/shard_map/pallas_call | solution.py:209
  39.4 1.1 %copy.6 = bf16[1,5,384,384]{3,2,1,0:T(8,128)(2,1)} copy(bf16[1,5,384,384]{3,2,1,0:T(8,128)(2,1)S(1)} %shard_map.46) | data formatting | bytes 2949120

commit v5 on v4

--- a/solution.py
+++ b/solution.py
@@ -11,7 +11,7 @@
 charge_steps = (0, 1, -1, 0, 0)
 W = len(charge_steps)
 ORDER = (1, 0, 3, 4, 2)
-DEPTH = 3
+DEPTH = 5
 
 
 def uses(w, t, x):

time: 40.7 us -> 40.7 us (level)
  no operation moved by 1% of the time
where the time goes in v5:
time: 40.7 us; the launch traced here: 40.5 us
  Pallas kernels  39.4 us (97%)
  local copies, waits for them, and re-layouts  1.11 us (3%)
    pallas_call x1, Pallas kernels, local(): pl.pallas_call(functools.partial(kernel, ns, nq), out_shape=pltpu.VMEM(en...  39.4 us
    unnamed x1, local copies, waits for them, and re-layouts  1.11 us

profile of v5, /device:TPU:28, one launch (start us, length us, event | category | flops | bytes accessed | tf_op | source)
XLA Modules:
  0.0 40.5 jit_solution(2563646157987568955)
XLA Ops:
  0.0 39.4 %shard_map.46 = bf16[1,5,384,384]{3,2,1,0:T(8,128)(2,1)S(1)} custom-call(bf16[1,2,384,384]{3,2,1,0:T(8,128)(2,1)} %site_hbm.1, bf16[1,5,384,384]{3,2,1,0:T(8,128)(2,1)} %env.1, f32[1,5,2,2,5]{4,3,2,1,0:T(2,128)} %bitcast.1, bf16[5,384,384]{2,1,0:T(8,128)(2,1)} %bnd.1), custom_call_target="tpu_custom_call" | custom-call | flops 3057647616 | bytes 17694720 | tf_op jit(solution)/shard_map/pallas_call | solution.py:209
  39.4 1.1 %copy.6 = bf16[1,5,384,384]{3,2,1,0:T(8,128)(2,1)} copy(bf16[1,5,384,384]{3,2,1,0:T(8,128)(2,1)S(1)} %shard_map.46) | data formatting | bytes 2949120

commit v6 on v5

--- a/solution.py
+++ b/solution.py
@@ -11,7 +11,7 @@
 charge_steps = (0, 1, -1, 0, 0)
 W = len(charge_steps)
 ORDER = (1, 0, 3, 4, 2)
-DEPTH = 5
+DEPTH = 2
 
 
 def uses(w, t, x):

time: 40.7 us -> 40.7 us (level); the launches traced: 40.5 us -> 39.9 us
  Pallas kernels: 39.4 us -> 38.8 us
    pallas_call x1, Pallas kernels: 39.4 us -> 38.8 us  [local(): pl.pallas_call(functools.partial(kernel, ns, nq), out_shape=pltpu.VMEM(en...]
where the time goes in v6:
time: 40.7 us; the launch traced here: 39.9 us
  Pallas kernels  38.8 us (95%)
  local copies, waits for them, and re-layouts  1.11 us (3%)
    pallas_call x1, Pallas kernels, local(): pl.pallas_call(functools.partial(kernel, ns, nq), out_shape=pltpu.VMEM(en...  38.8 us
    unnamed x1, local copies, waits for them, and re-layouts  1.11 us

profile of v6, /device:TPU:28, one launch (start us, length us, event | category | flops | bytes accessed | tf_op | source)
XLA Modules:
  0.0 39.9 jit_solution(12439779388740287884)
XLA Ops:
  0.0 38.8 %shard_map.46 = bf16[1,5,384,384]{3,2,1,0:T(8,128)(2,1)S(1)} custom-call(bf16[1,2,384,384]{3,2,1,0:T(8,128)(2,1)} %site_hbm.1, bf16[1,5,384,384]{3,2,1,0:T(8,128)(2,1)} %env.1, f32[1,5,2,2,5]{4,3,2,1,0:T(2,128)} %bitcast.1, bf16[5,384,384]{2,1,0:T(8,128)(2,1)} %bnd.1), custom_call_target="tpu_custom_call" | custom-call | flops 3057647616 | bytes 17694720 | tf_op jit(solution)/shard_map/pallas_call | solution.py:209
  38.8 1.1 %copy.6 = bf16[1,5,384,384]{3,2,1,0:T(8,128)(2,1)} copy(bf16[1,5,384,384]{3,2,1,0:T(8,128)(2,1)S(1)} %shard_map.46) | data formatting | bytes 2949120
